TPU v7x, 512 devices: a whole 4x4x16 slice. The times are simulated.
512 devices in a mesh: section: 16 (over z), dp: 32 (over x, y, core).
Axes of the slice: x: 4, y: 4, z: 16, core: 2. Of those that a mesh axis runs over, the one named last changes fastest.
Arguments:
- gradients: bfloat16 [176, 288, 4096], P('section', None, 'dp'), may hold values from -210000 to 210000
- momentum: float32 [176, 288, 4096], P('section', None, 'dp'), may hold values from -60 to 60
Outputs:
- new_momentum: float32 [176, 288, 4096], P('section', None, 'dp')
- orthogonal_update: bfloat16 [176, 288, 4096], P('section', None, 'dp')
All inputs are finite; a program needn't handle non-finite values.
Results may differ from a plain program's by a relative error of at most 0.0049.
Values may be sent and summed in bfloat16 or wider, within the bound.
A program may use at most 64 MiB of HBM per device.

v0:
```python
import math

import jax
import jax.numpy as jnp
from jax import lax
from jax.sharding import PartitionSpec as P

ITERS = 2


momentum_decay = 0.95
quintic_one = 3.4445
quintic_two = -4.775
quintic_three = 2.0315


def per_device(gradients, momentum):
    dp_count = lax.axis_size("dp")
    mat_count, row_count, shard_cols = gradients.shape
    full_width = shard_cols * dp_count
    entries = mat_count * lax.axis_size("section") * row_count * full_width
    grad_float = gradients.astype(jnp.float32)
    total = lax.psum(jnp.sum(grad_float * grad_float), ("section", "dp"))
    clip_factor = jnp.minimum(1.0, lax.rsqrt(total / entries + 1e-06))
    scaled = grad_float * clip_factor
    new_momentum = momentum_decay * momentum + scaled
    prepared = (scaled + momentum_decay * new_momentum).astype(jnp.bfloat16)
    group_size = 1
    group_count = dp_count // group_size
    slot_count = -(-mat_count // group_count)
    piece_cols = shard_cols // group_size
    padded = jnp.pad(prepared, ((0, group_count * slot_count - mat_count), (0, 0), (0, 0)))
    arranged = padded.reshape(group_count, slot_count, row_count, group_size, piece_cols)
    outgoing = jnp.transpose(arranged, (0, 3, 1, 2, 4)).reshape(
        dp_count, slot_count, row_count, piece_cols
    )
    width_scale = math.sqrt(max(row_count, full_width))
    matrices = lax.all_to_all(outgoing, "dp", split_axis=0, concat_axis=3, tiled=True)[0].astype(
        jnp.float32
    )
    squares = jnp.sum(matrices * matrices, axis=(1, 2))
    matrices = matrices / (jnp.sqrt(squares) + 1e-07)[:, None, None]
    for sweep_index in range(ITERS):
        gram_mat = jnp.einsum(
            "krw,ksw->krs",
            matrices,
            matrices,
            precision=lax.Precision.HIGHEST,
            preferred_element_type=jnp.float32,
        )
        squared = jnp.einsum(
            "krs,kst->krt",
            gram_mat,
            gram_mat,
            precision=lax.Precision.HIGHEST,
            preferred_element_type=jnp.float32,
        )
        poly_mat = quintic_two * gram_mat + quintic_three * squared
        matrices = quintic_one * matrices + jnp.einsum(
            "krs,ksw->krw",
            poly_mat,
            matrices,
            precision=lax.Precision.HIGHEST,
            preferred_element_type=jnp.float32,
        )
    ortho_owned = (width_scale * matrices).astype(jnp.bfloat16)[None]
    returned = lax.all_to_all(ortho_owned, "dp", split_axis=3, concat_axis=0, tiled=True)
    regrouped = returned.reshape(group_count, group_size, slot_count, row_count, piece_cols)
    restored = jnp.transpose(regrouped, (0, 2, 3, 1, 4)).reshape(
        group_count * slot_count, row_count, shard_cols
    )
    return (new_momentum, restored[:mat_count])


def solution(mesh):
    placed = (P("section", None, "dp"), P("section", None, "dp"))
    return jax.shard_map(
        per_device,
        mesh=mesh,
        in_specs=placed,
        out_specs=(P("section", None, "dp"), P("section", None, "dp")),
        check_vma=False,
    )
```

profile of v0, /device:TPU:1, one launch (start us, length us, event | category | flops | bytes accessed | tf_op | source)
XLA Modules:
  0.0 399.7 jit_solution(14089326230418106468)
XLA Ops:
  0.6 2.2 fusion.12
  2.8 111.0 %psum.7 = f32[]{:T(128)} all-reduce(f32[]{:T(128)} %fusion.12), channel_id=1, replica_groups=mesh['section'=16,'dp'=32] {'section','dp'}, use_global_device_ids=true, to_apply=%region_1.0 | all-reduce | flops 1 | bytes 8 | tf_op jit(solution)/shard_map/psum | solution.py:23
  114.5 3.2 fusion.11
  117.7 0.3 pad_bitcast_fusion
  118.0 35.4 %all_to_all.24 = bf16[32,1,288,128]{3,2,1,0:T(8,128)(2,1)S(1)} all-to-all(bf16[32,1,288,128]{3,2,1,0:T(8,128)(2,1)S(1)} %pad_bitcast_fusion), channel_id=1, replica_groups=mesh['section'=16,'dp'=32] {'dp'}, dimensions={0} | all-to-all | bytes 4718592 | tf_op jit(solution)/shard_map/all_to_all | solution.py:38
  153.3 1.8 fusion.3
  155.8 55.9 %fusion.14 = f32[288,288]{1,0:T(8,128)S(1)} fusion(f32[]{:T(128)S(6)} %add.36, bf16[32,1,288,128]{3,2,1,0:T(8,128)(2,1)S(1)} %all_to_all.24), kind=kOutput, calls=%fused_computation.22 | convolution fusion | flops 4079222784 | bytes 2691076 | tf_op jit(solution)/shard_map/krw,ksw->krs/dot_general | solution.py:44
  211.7 1.0 fusion.18
  212.7 0.6 fusion.13
  213.3 2.7 copy.15
  216.0 0.6 fusion.8
  216.7 2.7 copy.14
  219.4 11.9 %convolution_add_fusion.1 = f32[288,4096]{1,0:T(8,128)S(1)} fusion(f32[288,288]{1,0:T(8,128)S(1)} %fusion.18, f32[36,8,32,128]{3,2,1,0:T(8,128)S(1)} %bitcast.65, f32[36,8,32,128]{3,2,1,0:T(8,128)S(1)} %bitcast.62), kind=kOutput, calls=%fused_computation.4 | convolution fusion | flops 4078043136 | bytes 14487552 | tf_op jit(solution)/shard_map/krs,ksw->krw/dot_general | solution.py:59
  231.4 7.8 %fusion.20 = f32[288,288]{1,0:T(8,128)S(1)} fusion(f32[288,4096]{1,0:T(8,128)S(1)} %convolution_add_fusion.1), kind=kOutput, calls=%fused_computation.28 | convolution fusion | flops 4076863488 | bytes 5050368 | tf_op jit(solution)/shard_map/krw,ksw->krs/dot_general | solution.py:44
  239.2 1.0 fusion.17
  240.2 8.0 %fusion.2 = bf16[1,1,288,4096]{3,2,1,0:T(8,128)(2,1)S(1)} fusion(f32[288,288]{1,0:T(8,128)S(1)} %fusion.17, f32[288,4096]{1,0:T(8,128)S(1)} %convolution_add_fusion.1), kind=kOutput, calls=%fused_computation.6 | convolution fusion | flops 4081582080 | bytes 7409664 | tf_op jit(solution)/shard_map/krs,ksw->krw/dot_general | solution.py:59
  248.2 12.1 %copy.16 = bf16[1,1,288,4096]{2,1,0,3:T(2,128)(2,1)} copy(bf16[1,1,288,4096]{3,2,1,0:T(8,128)(2,1)S(1)} %fusion.2) | data formatting | bytes 4718592 | tf_op jit(solution)/shard_map/broadcast_in_dim | solution.py:66
  260.3 0.5 broadcast.60
  260.8 67.3 %reduce.4 = bf16[4096,288]{1,0:T(8,128)(2,1)S(1)} reduce(bf16[4096,1,1,288]{3,2,1,0:T(2,128)(2,1)} %bitcast.63, bf16[]{:T(256)} %broadcast.60), dimensions={1,2}, to_apply=%bitcast.51.reduce_sub_computation | reduce | bytes 4718594
  328.1 5.4 %reshape.85 = bf16[32,2,18432]{2,1,0:T(2,128)(2,1)} reshape(bf16[4096,288]{1,0:T(8,128)(2,1)S(1)} %reduce.4) | data formatting | bytes 4718592
  333.5 35.5 %all_to_all.25 = bf16[32,2,18432]{2,1,0:T(2,128)(2,1)S(1)} all-to-all(bf16[32,2,18432]{2,1,0:T(2,128)(2,1)} %reshape.85), channel_id=1, replica_groups=mesh['section'=16,'dp'=32] {'dp'}, dimensions={0} | all-to-all | bytes 4718592 | tf_op jit(solution)/shard_map/all_to_all | solution.py:67
  368.9 14.0 %reshape.86 = bf16[4096,1,1,288]{3,2,1,0:T(2,128)(2,1)} reshape(bf16[32,2,18432]{2,1,0:T(2,128)(2,1)S(1)} %all_to_all.25) | data formatting | bytes 4718592
  382.9 14.7 %copy.17 = bf16[1,1,288,4096]{3,2,1,0:T(8,128)(2,1)S(1)} copy(bf16[1,1,288,4096]{2,1,0,3:T(2,128)(2,1)} %bitcast.64) | data formatting | bytes 4718592 | tf_op jit(solution)/shard_map/all_to_all | solution.py:67
  397.6 0.5 copy.21
  398.1 0.2 slice_bitcast_fusion
  398.3 1.1 copy.18
where the time goes:
time: 403 us; the launch traced here: 400 us
  blocking collectives  182 us (45%)
  matrix products  85.6 us (21%)
  other arithmetic  75.7 us (19%)
  local copies, waits for them, and re-layouts  54.1 us (13%)
    psum x1, blocking collectives, per_device(): total = lax.psum(jnp.sum(grad_float * grad_float), ('section', 'dp'))  111 us
    unnamed x1, other arithmetic  67.3 us
    dot_general x2, matrix products, per_device(): jnp.einsum('krw,ksw->krs', matrices, matrices, precision=lax.Precision.HI...  63.7 us
    all_to_all x1, blocking collectives, per_device(): lax.all_to_all(ortho_owned, 'dp', split_axis=3, concat_axis=0, tiled=True)  35.5 us
    all_to_all x1, blocking collectives, per_device(): lax.all_to_all(outgoing, 'dp', split_axis=0, concat_axis=3, tiled=True)[0]  35.4 us
    unnamed x5, local copies, waits for them, and re-layouts  21.5 us
    dot_general x2, matrix products, per_device(): jnp.einsum('krs,ksw->krw', poly_mat, matrices, precision=lax.Precision.HI...  19.9 us
    all_to_all x1, local copies, waits for them, and re-layouts, per_device(): lax.all_to_all(ortho_owned, 'dp', split_axis=3, concat_axis=0, tiled=True)  14.7 us

commit v1 on v0

v1 whole, which is shorter than its diff:
```python
import jax
import jax.numpy as jnp
from jax import lax
from jax.experimental import pallas as pl
from jax.experimental.pallas import tpu as pltpu
from jax.sharding import PartitionSpec as P

MATS = 11
ROWS = 288
COLS = 128
HALF = 6
PACK = 352
PART = 176
ENTRIES = 176 * 288 * 4096
WIDTH_SCALE = 64.0

DECAY = 0.95
ONE = 3.4445
TWO = -4.775
THREE = 2.0315

F32 = jnp.float32
BF16 = jnp.bfloat16
MESH = pl.DeviceIdType.MESH


def dot(a, b):
    return jnp.dot(a, b, preferred_element_type=F32)


def dot_nt(a, b):
    return lax.dot_general(a, b, (((1,), (1,)), ((), ())), preferred_element_type=F32)


def split(a):
    high = a.astype(BF16)
    return high, (a - high.astype(F32)).astype(BF16)


def product(a, b):
    wide, tail = slice(0, 256), slice(256, 288)
    left = jnp.concatenate(
        [a[0][:, wide], a[0][:, wide], a[1][:, wide], a[0][:, tail], a[0][:, tail], a[1][:, tail]], axis=1
    )
    right = jnp.concatenate([b[0][wide], b[1][wide], b[0][wide], b[0][tail], b[1][tail], b[0][tail]], axis=0)
    main = dot(left, right[:, wide])
    corner = dot(left[tail], right[:, tail])
    side = jnp.concatenate([main[tail].T, corner], axis=0)
    return jnp.concatenate([main, side], axis=1)


def triangle():
    row = lax.broadcasted_iota(jnp.int32, (128, 128), 0)
    col = lax.broadcasted_iota(jnp.int32, (128, 128), 1)
    return row, col


def pack(first, cross, second, low):
    row, col = triangle()
    middle = jnp.sum(jnp.where(row == col, second, 0.0), axis=0, keepdims=True)
    rest = jnp.concatenate([middle[:, 96:128], jnp.zeros((1, 64), F32)], axis=1)
    beside = jnp.concatenate(
        [jnp.broadcast_to(middle[:, 0:96], (16, 96)), jnp.broadcast_to(rest, (16, 96))], axis=0
    )
    corner = jnp.concatenate([low[:, 256:288], beside], axis=1)
    return (
        (0, jnp.where(col >= row, first, second)),
        (128, cross),
        (256, low[:, :128]),
        (288, low[:, 128:256]),
        (320, corner),
    )


def unpack(full, both, cross, low0, low1, corner):
    row, col = triangle()
    middle = jnp.concatenate([corner[0:1, 32:128], corner[16:17, 32:64]], axis=1)
    turned = both.T
    low = jnp.concatenate([low0, low1], axis=1)
    full[0:128, 0:128] = jnp.where(col >= row, both, turned)
    full[0:128, 128:256] = cross
    full[128:256, 0:128] = cross.T
    full[128:256, 128:256] = jnp.where(
        row == col, jnp.broadcast_to(middle, (128, 128)), jnp.where(row > col, both, turned)
    )
    full[256:288, 0:256] = low
    full[0:256, 256:288] = low.T
    full[256:288, 256:288] = corner[:, :32]


def kernel(
    g_hbm,
    m_hbm,
    nm_out,
    o_hbm,
    gbuf,
    mbuf,
    nmbuf,
    acc,
    accz,
    accp,
    gx,
    mx,
    xx,
    gloc,
    gtx,
    r1,
    s2,
    r2,
    gf,
    qbuf,
    obuf,
    g_sem,
    m_sem,
    nm_sem,
    z_send,
    z_recv,
    p_send,
    p_recv,
    x_send,
    x_recv,
    mx_send,
    mx_recv,
    s1_send,
    s1_recv,
    s2_send,
    s2_recv,
    q1_send,
    q2_send,
    q_recv,
    o_send,
    o_recv,
    ol_sem,
    relay,
):
    z = lax.axis_index("section")
    d = lax.axis_index("dp")
    x = d // 8
    y = (d // 2) % 4
    c = d % 2

    def dev(px, py, pc):
        return (z, (px * 4 + py) * 2 + pc)

    partner = dev(x, y, 1 - c)

    def remote(src, dst, send, recv, target):
        return pltpu.make_async_remote_copy(
            src_ref=src, dst_ref=dst, send_sem=send, recv_sem=recv, device_id=target, device_id_type=MESH
        )

    def load_g(i):
        return pltpu.make_async_copy(g_hbm.at[i], gbuf.at[i], g_sem.at[i])

    def store_nm(i):
        return pltpu.make_async_copy(nmbuf.at[i], nm_out.at[i], nm_sem.at[i])

    def load_m(i):
        return pltpu.make_async_copy(m_hbm.at[i], mbuf.at[i], m_sem.at[i])

    @pl.loop(0, MATS)
    def _(i):
        load_g(i).start()

    barrier = pltpu.get_barrier_semaphore()

    def greet(target):
        pl.semaphore_signal(barrier, inc=1, device_id=target, device_id_type=MESH)

    @pl.loop(1, 5)
    def _(o):
        greet((lax.rem(z + o, 16), d))
        greet((lax.rem(z + 16 - o, 16), d))

    @pl.loop(1, 16)
    def _(o):
        greet(dev((x + o // 4) % 4, (y + o) % 4, c))

    greet(partner)

    def squares(i, total):
        load_g(i).wait()
        value = gbuf[i].astype(F32)
        return total + jnp.sum((value * value).reshape(ROWS // 8, 8, COLS), axis=0)

    total = lax.fori_loop(0, MATS, squares, jnp.zeros((8, COLS), F32))
    acc[0, 0:1] = jnp.sum(total, axis=0, keepdims=True)

    @pl.loop(0, MATS)
    def _(i):
        load_m(i).start()

    pl.semaphore_wait(barrier, 24)

    pl.semaphore_signal(relay.at[0], inc=1, device_id=(lax.rem(z + 4, 16), d), device_id_type=MESH)
    pl.semaphore_signal(relay.at[1], inc=1, device_id=(lax.rem(z + 12, 16), d), device_id_type=MESH)

    def core_copy():
        return remote(
            acc.at[0, pl.ds(0, 1)], accp.at[15, pl.ds(0, 1)], p_send.at[15], p_recv.at[15], partner
        )

    core_copy().start()
    core_copy().wait_recv()
    acc[1, 0:1] = acc[0, 0:1] + accp[15, 0:1]

    def p_copy(o):
        return remote(
            acc.at[1, pl.ds(0, 1)],
            accp.at[o - 1, pl.ds(0, 1)],
            p_send.at[o - 1],
            p_recv.at[o - 1],
            dev((x + o // 4) % 4, (y + o) % 4, c),
        )

    @pl.loop(1, 16)
    def _(o):
        p_copy(o).start()

    def gx_copy(j):
        return remote(gbuf.at[HALF * (1 - c) + j], gx.at[j], x_send.at[j], x_recv.at[j], partner)

    def mx_copy(j):
        return remote(mbuf.at[HALF * (1 - c) + j], mx.at[j], mx_send.at[j], mx_recv.at[j], partner)

    @pl.loop(0, MATS)
    def _(i):
        load_m(i).wait()

    @pl.loop(0, HALF)
    def _(j):
        @pl.when(HALF * (1 - c) + j < MATS)
        def _():
            gx_copy(j).start()
            mx_copy(j).start()

    pl.semaphore_wait(relay.at[0], 1)
    pl.semaphore_wait(relay.at[1], 1)

    @pl.loop(1, 16)
    def _(o):
        p_copy(o).wait_recv()

    acc[2, 0:1] = acc[1, 0:1] + jnp.sum(accp[0:15, 0:1, :], axis=0)

    def z_copy(o):
        return remote(
            acc.at[2, pl.ds(0, 1)],
            accz.at[o - 1, pl.ds(0, 1)],
            z_send.at[o - 1],
            z_recv.at[o - 1],
            (lax.rem(z + o, 16), d),
        )

    @pl.loop(1, 16)
    def _(o):
        z_copy(o).start()

    @pl.loop(1, 16)
    def _(o):
        z_copy(o).wait_recv()

    mean = jnp.sum(acc[2, 0:1] + jnp.sum(accz[:, 0:1, :], axis=0), keepdims=True) / ENTRIES + 1e-06
    root = lax.rsqrt(mean)
    root = root * (1.5 - 0.5 * mean * root * root)
    clip = jnp.minimum(1.0, root)

    def prepare(gradient, moment):
        scaled = gradient.astype(F32) * clip
        return (scaled + DECAY * (DECAY * moment + scaled)).astype(BF16)

    def owner(j):
        m = HALF * c + j
        return m < MATS, m % 4, (m // 4 + m % 4) % 4

    def slot(own, at):
        return jnp.maximum((own - at + 4) % 4 - 1, 0)

    def scale(px, py):
        return jnp.broadcast_to((16 + px * 4 + py).astype(F32) * 0.0625, (1, COLS))

    def s1_x(j, xm):
        k = slot(x, xm)
        return remote(
            gtx.at[j, pl.ds(0, PART)], r1.at[0, j, k], s1_send.at[0, j], s1_recv.at[0, j, k], dev(xm, y, c)
        )

    def s1_y(j, ym):
        k = slot(y, ym)
        return remote(
            gtx.at[j, pl.ds(PART, PART)], r1.at[1, j, k], s1_send.at[1, j], s1_recv.at[1, j, k], dev(x, ym, c)
        )

    @pl.loop(0, HALF)
    def _(j):
        real, xm, ym = owner(j)

        @pl.when(real)
        def _():
            m = HALF * c + j
            remote(gx.at[j], gx.at[j], x_send.at[j], x_recv.at[j], partner).wait_recv()
            remote(mx.at[j], mx.at[j], mx_send.at[j], mx_recv.at[j], partner).wait_recv()
            xx[j, 0] = prepare(gbuf[m], mbuf[m])
            xx[j, 1] = prepare(gx[j], mx[j])
            value = jnp.concatenate([xx[j, 0], xx[j, 1]], axis=1)
            top = dot_nt(value[:128], value[:256])
            mid = dot_nt(value[128:256], value[128:256])
            low = dot_nt(value[256:288], value)
            pieces = pack(top[:, :128], top[:, 128:], mid, low)
            own_scale = scale(x, y)
            for at, piece in pieces:
                gloc[j, at : at + piece.shape[0]] = piece
                gtx[j, at : at + piece.shape[0]] = (piece * own_scale).astype(BF16)

            @pl.when(xm != x)
            def _():
                s1_x(j, xm).start()

            @pl.when(ym != y)
            def _():
                s1_y(j, ym).start()

    @pl.loop(0, MATS)
    def _(i):
        nmbuf[i] = DECAY * mbuf[i] + gbuf[i].astype(F32) * clip
        store_nm(i).start()

    def s2_x(j, ym):
        k = slot(y, ym)
        return remote(s2.at[0, j], r2.at[0, k], s2_send.at[0, j], s2_recv.at[0, k], dev(x, ym, c))

    def s2_y(j, xm):
        k = slot(x, xm)
        return remote(s2.at[1, j], r2.at[1, k], s2_send.at[1, j], s2_recv.at[1, k], dev(xm, y, c))

    def wait_r1(half, j, k):
        remote(r1.at[half, j, k], r1.at[half, j, k], s1_send.at[half, j], s1_recv.at[half, j, k], partner).wait_recv()

    def wait_r2(half, k):
        remote(r2.at[half, k], r2.at[half, k], s2_send.at[half, 0], s2_recv.at[half, k], partner).wait_recv()

    @pl.loop(0, HALF)
    def _(j):
        real, xm, ym = owner(j)

        def reduce(half, near, far, start):
            @pl.when(real & near)
            def _():
                for k in range(3):
                    wait_r1(half, j, k)
                total = gloc[j, PART * half : PART * half + PART]
                for k in range(3):
                    from_x = (x + k + 1) % 4 if half == 0 else x
                    from_y = y if half == 0 else (y + k + 1) % 4
                    total = total + r1[half, j, k].astype(F32) * (1.0 / scale(from_x, from_y))
                gloc[j, PART * half : PART * half + PART] = total

                @pl.when(far)
                def _():
                    s2[half, j] = (total * scale(x, y)).astype(BF16)
                    start()

        reduce(0, xm == x, ym != y, lambda: s2_x(j, ym).start())
        reduce(1, ym == y, xm != x, lambda: s2_y(j, xm).start())

    def q1_copy(j, half, k, o):
        target = dev(x, (y + o) % 4, c) if half == 0 else dev((x + o) % 4, y, c)
        return remote(
            qbuf.at[j, half, k], qbuf.at[j, half, k], q1_send.at[half, k, o - 1], q_recv.at[j, half, k], target
        )

    def q2_copy(j, half, k, o):
        target = dev((x + o) % 4, y, c) if half == 0 else dev(x, (y + o) % 4, c)
        return remote(
            qbuf.at[j, half, k], qbuf.at[j, half, k], q2_send.at[j, half, k, o - 1], q_recv.at[j, half, k], target
        )

    @pl.loop(0, HALF)
    def _(j):
        real, xm, ym = owner(j)

        @pl.when(real & (xm == x) & (ym == y))
        def _():
            for half in range(2):
                for k in range(3):
                    wait_r2(half, k)
                total = gloc[j, PART * half : PART * half + PART]
                for k in range(3):
                    from_x = x if half == 0 else (x + k + 1) % 4
                    from_y = (y + k + 1) % 4 if half == 0 else y
                    total = total + r2[half, k].astype(F32) * (1.0 / scale(from_x, from_y))
                gloc[j, PART * half : PART * half + PART] = total
            unpack(
                gf,
                gloc[j, 0:128],
                gloc[j, 128:256],
                gloc[j, 256:288],
                gloc[j, 288:320],
                gloc[j, 320:352],
            )
            row = lax.broadcasted_iota(jnp.int32, (ROWS, ROWS), 0)
            col = lax.broadcasted_iota(jnp.int32, (ROWS, ROWS), 1)
            diag = row == col
            raw = gf[...]
            norm = jnp.sqrt(jnp.sum(jnp.where(diag, raw, 0.0), keepdims=True)) + 1e-07
            inverse = 1.0 / norm
            gram = raw * (inverse * inverse)
            gram_s = split(gram)
            poly = TWO * gram + THREE * product(gram_s, gram_s) + jnp.where(diag, ONE, 0.0)
            poly_s = split(poly)
            left_s = split(product(poly_s, gram_s))
            gram = product(left_s, poly_s)
            gram_s = split(gram)
            last = TWO * gram + THREE * product(gram_s, gram_s) + jnp.where(diag, ONE, 0.0)
            gf[...] = product(split(last), poly_s) * (WIDTH_SCALE * inverse)

            pieces = pack(gf[0:128, 0:128], gf[0:128, 128:256], gf[128:256, 128:256], gf[256:288, :])
            for at, piece in pieces:
                both = split(piece)
                size = piece.shape[0]
                for half in range(2):
                    lo = max(at, PART * half)
                    hi = min(at + size, PART * half + PART)
                    if lo < hi:
                        for k in range(2):
                            qbuf[j, half, k, lo - PART * half : hi - PART * half] = both[k][lo - at : hi - at]
            for k in range(2):
                for half in range(2):
                    for o in (2, 1, 3):
                        q1_copy(j, half, k, o).start()

    def wait_q(j, half, k):
        remote(
            qbuf.at[j, half, k], qbuf.at[j, half, k], q1_send.at[half, k, 0], q_recv.at[j, half, k], partner
        ).wait_recv()

    @pl.loop(0, HALF)
    def _(j):
        real, xm, ym = owner(j)

        def forward(half, k, near, far):
            @pl.when(real & near)
            def _():
                @pl.when(far)
                def _():
                    wait_q(j, half, k)

                for o in (2, 1, 3):
                    q2_copy(j, half, k, o).start()

        for k in range(2):
            forward(0, k, xm == x, ym != y)
            forward(1, k, ym == y, xm != x)

    @pl.loop(0, MATS)
    def _(i):
        store_nm(i).wait()

    @pl.loop(1, 16)
    def _(o):
        z_copy(o).wait_send()
        p_copy(o).wait_send()

    core_copy().wait_send()

    @pl.loop(0, HALF)
    def _(j):
        real, xm, ym = owner(j)

        @pl.when(HALF * (1 - c) + j < MATS)
        def _():
            gx_copy(j).wait_send()
            mx_copy(j).wait_send()

        @pl.when(real)
        def _():
            @pl.when(xm != x)
            def _():
                s1_x(j, xm).wait_send()

            @pl.when(ym != y)
            def _():
                s1_y(j, ym).wait_send()

            @pl.when((xm == x) & (ym != y))
            def _():
                s2_x(j, ym).wait_send()

            @pl.when((ym == y) & (xm != x))
            def _():
                s2_y(j, xm).wait_send()

    def o_copy(j):
        m = HALF * c + j
        return remote(obuf.at[j, 1], o_hbm.at[m], o_send.at[j], o_recv.at[j], partner)

    def o_local(j):
        m = HALF * c + j
        return pltpu.make_async_copy(obuf.at[j, 0], o_hbm.at[m], ol_sem.at[j])

    @pl.loop(0, HALF)
    def _(j):
        real, xm, ym = owner(j)

        @pl.when(real)
        def _():
            @pl.when(xm != x)
            def _():
                wait_q(j, 0, 0)
                wait_q(j, 0, 1)

            @pl.when(ym != y)
            def _():
                wait_q(j, 1, 0)
                wait_q(j, 1, 1)

            first = qbuf[j, 0, 0].astype(F32) + qbuf[j, 0, 1].astype(F32)
            second = qbuf[j, 1, 0].astype(F32) + qbuf[j, 1, 1].astype(F32)
            cross = jnp.concatenate([first[128:176], second[0:80]], axis=0)
            unpack(gf, first[0:128], cross, second[80:112], second[112:144], second[144:176])
            full = split(gf[...])
            value = jnp.concatenate([xx[j, 0], xx[j, 1]], axis=1)
            result = (dot(full[0], value) + dot(full[1], value)).astype(BF16)
            obuf[j, 0] = result[:, :128]
            obuf[j, 1] = result[:, 128:]
            o_local(j).start()
            o_copy(j).start()

    @pl.loop(0, HALF)
    def _(j):
        real, xm, ym = owner(j)

        @pl.when(real & (xm == x) & (ym == y))
        def _():
            for k in range(2):
                for half in range(2):
                    for o in range(1, 4):
                        q1_copy(j, half, k, o).wait_send()

        @pl.when(real & (xm == x))
        def _():
            for k in range(2):
                for o in range(1, 4):
                    q2_copy(j, 0, k, o).wait_send()

        @pl.when(real & (ym == y))
        def _():
            for k in range(2):
                for o in range(1, 4):
                    q2_copy(j, 1, k, o).wait_send()

    @pl.loop(0, HALF)
    def _(j):
        @pl.when(HALF * (1 - c) + j < MATS)
        def _():
            remote(obuf.at[j, 1], obuf.at[j, 1], o_send.at[j], o_recv.at[j], partner).wait_recv()

        @pl.when(HALF * c + j < MATS)
        def _():
            o_local(j).wait()
            o_copy(j).wait_send()


def per_device(gradients, momentum):
    dma = pltpu.SemaphoreType.DMA
    vmem = pltpu.VMEM
    any_spec = pl.BlockSpec(memory_space=pl.ANY)
    return pl.pallas_call(
        kernel,
        out_shape=(
            jax.ShapeDtypeStruct((MATS, ROWS, COLS), F32),
            jax.ShapeDtypeStruct((MATS, ROWS, COLS), BF16),
        ),
        in_specs=[pl.BlockSpec(memory_space=pltpu.HBM)] * 2,
        out_specs=(any_spec, any_spec),
        scratch_shapes=[
            vmem((MATS, ROWS, COLS), BF16),
            vmem((MATS, ROWS, COLS), F32),
            vmem((MATS, ROWS, COLS), F32),
            vmem((3, 8, COLS), F32),
            vmem((15, 8, COLS), F32),
            vmem((16, 8, COLS), F32),
            vmem((HALF, ROWS, COLS), BF16),
            vmem((HALF, ROWS, COLS), F32),
            vmem((HALF, 2, ROWS, COLS), BF16),
            vmem((HALF, PACK, COLS), F32),
            vmem((HALF, PACK, COLS), BF16),
            vmem((2, HALF, 3, PART, COLS), BF16),
            vmem((2, HALF, PART, COLS), BF16),
            vmem((2, 3, PART, COLS), BF16),
            vmem((ROWS, ROWS), F32),
            vmem((HALF, 2, 2, PART, COLS), BF16),
            vmem((HALF, 2, ROWS, COLS), BF16),
            dma((MATS,)),
            dma((MATS,)),
            dma((MATS,)),
            dma((15,)),
            dma((15,)),
            dma((16,)),
            dma((16,)),
            dma((HALF,)),
            dma((HALF,)),
            dma((HALF,)),
            dma((HALF,)),
            dma((2, HALF)),
            dma((2, HALF, 3)),
            dma((2, HALF)),
            dma((2, 3)),
            dma((2, 2, 3)),
            dma((HALF, 2, 2, 3)),
            dma((HALF, 2, 2)),
            dma((HALF,)),
            dma((HALF,)),
            dma((HALF,)),
            pltpu.SemaphoreType.REGULAR((2,)),
        ],
        compiler_params=pltpu.CompilerParams(
            collective_id=0, has_side_effects=True, vmem_limit_bytes=40 * 1024 * 1024
        ),
        cost_estimate=pl.CostEstimate(flops=1500000000, bytes_accessed=5000000, transcendentals=0),
        name="muon",
    )(
        pltpu.with_memory_space_constraint(gradients, pltpu.HBM),
        pltpu.with_memory_space_constraint(momentum, pltpu.HBM),
    )


def solution(mesh):
    placed = (P("section", None, "dp"), P("section", None, "dp"))
    return jax.shard_map(
        per_device, mesh=mesh, in_specs=placed, out_specs=placed, check_vma=False
    )
```

time: 403 us -> 60.7 us (0.15)
  blocking collectives: 182 us -> 0 us
  matrix products: 85.6 us -> 0 us
  other arithmetic: 75.7 us -> 0 us
  Pallas kernels: 0 us -> 57.8 us
  local copies, waits for them, and re-layouts: 54.1 us -> 2.05 us
    psum x1 -> x0, blocking collectives: 111 us -> none  [per_device(): total = lax.psum(jnp.sum(grad_float * grad_float), ('section', 'dp'))]
    dot_general x6 -> x0, matrix products: 85.6 us -> none  [the longest x2 63.7 us: per_device(): jnp.einsum('krw,ksw->krs', matrices, matrices, precision=lax.Precision.HI...]
    all_to_all x2 -> x0, blocking collectives: 70.8 us -> none  [the longest x1 35.5 us: per_device(): lax.all_to_all(ortho_owned, 'dp', split_axis=3, concat_axis=0, tiled=True)]
    unnamed x1 -> x0, other arithmetic: 67.3 us -> none
    pallas_call x0 -> x1, Pallas kernels: none -> 57.8 us  [per_device(): pl.pallas_call(kernel, out_shape=(jax.ShapeDtypeStruct((MATS, ROWS, COLS)...]
    unnamed x5 -> x2, local copies, waits for them, and re-layouts: 21.5 us -> 2.05 us
    all_to_all x1 -> x0, local copies, waits for them, and re-layouts: 14.7 us -> none  [per_device(): lax.all_to_all(ortho_owned, 'dp', split_axis=3, concat_axis=0, tiled=True)]
    broadcast_in_dim x1 -> x0, local copies, waits for them, and re-layouts: 12.1 us -> none  [per_device(): ortho_owned = (width_scale * matrices).astype(jnp.bfloat16)[None]]
where the time goes in v1:
time: 60.7 us; the launch traced here: 60.5 us
  Pallas kernels  57.8 us (95%)
  local copies, waits for them, and re-layouts  2.05 us (3%)
  between operations  0.64 us (1%)
    pallas_call x1, Pallas kernels, per_device(): pl.pallas_call(kernel, out_shape=(jax.ShapeDtypeStruct((MATS, ROWS, COLS)...  57.8 us
    unnamed x2, local copies, waits for them, and re-layouts  2.05 us

profile of v1, /device:TPU:1, one launch (start us, length us, event | category | flops | bytes accessed | tf_op | source)
XLA Modules:
  0.0 60.5 jit_solution(3959681780571760640)
XLA Ops:
  0.6 57.8 %muon.1 = (f32[11,288,128]{2,1,0:T(8,128)S(1)}, bf16[11,288,128]{2,1,0:T(8,128)(2,1)S(1)}) custom-call(bf16[11,288,128]{2,1,0:T(8,128)(2,1)} %g_hbm.1, f32[11,288,128]{2,1,0:T(8,128)} %m_hbm.1), custom_call_target="tpu_custom_call" | custom-call | flops 1500000000 | bytes 5000000 | tf_op jit(solution)/shard_map/muon/pallas_call | solution.py:568
  58.4 1.2 %copy.6 = f32[11,288,128]{2,1,0:T(8,128)} copy(f32[11,288,128]{2,1,0:T(8,128)S(1)} %get-tuple-element.4) | data formatting | bytes 3244032
  59.6 0.9 %copy.7 = bf16[11,288,128]{2,1,0:T(8,128)(2,1)} copy(bf16[11,288,128]{2,1,0:T(8,128)(2,1)S(1)} %get-tuple-element.5) | data formatting | bytes 1622016

commit v2 on v1

--- a/solution.py
+++ b/solution.py
@@ -434,23 +434,24 @@
             qbuf.at[j, half, k], qbuf.at[j, half, k], q1_send.at[half, k, 0], q_recv.at[j, half, k], partner
         ).wait_recv()
 
-    @pl.loop(0, HALF)
-    def _(j):
-        real, xm, ym = owner(j)
-
-        def forward(half, k, near, far):
-            @pl.when(real & near)
-            def _():
-                @pl.when(far)
+    for k in range(2):
+
+        @pl.loop(0, HALF)
+        def _(j):
+            real, xm, ym = owner(j)
+
+            def forward(half, near, far):
+                @pl.when(real & near)
                 def _():
-                    wait_q(j, half, k)
-
-                for o in (2, 1, 3):
-                    q2_copy(j, half, k, o).start()
-
-        for k in range(2):
-            forward(0, k, xm == x, ym != y)
-            forward(1, k, ym == y, xm != x)
+                    @pl.when(far)
+                    def _():
+                        wait_q(j, half, k)
+
+                    for o in (2, 1, 3):
+                        q2_copy(j, half, k, o).start()
+
+            forward(0, xm == x, ym != y)
+            forward(1, ym == y, xm != x)
 
     @pl.loop(0, MATS)
     def _(i):

time: 60.7 us -> 59.5 us (0.980)
  Pallas kernels: 57.8 us -> 56.7 us
    pallas_call x1, Pallas kernels: 57.8 us -> 56.7 us  [per_device(): pl.pallas_call(kernel, out_shape=(jax.ShapeDtypeStruct((MATS, ROWS, COLS)...]
where the time goes in v2:
time: 59.5 us; the launch traced here: 59.3 us
  Pallas kernels  56.7 us (95%)
  local copies, waits for them, and re-layouts  2.05 us (3%)
  between operations  0.64 us (1%)
    pallas_call x1, Pallas kernels, per_device(): pl.pallas_call(kernel, out_shape=(jax.ShapeDtypeStruct((MATS, ROWS, COLS)...  56.7 us
    unnamed x2, local copies, waits for them, and re-layouts  2.05 us

profile of v2, /device:TPU:1, one launch (start us, length us, event | category | flops | bytes accessed | tf_op | source)
XLA Modules:
  0.0 59.3 jit_solution(6209120289692616056)
XLA Ops:
  0.6 56.7 %muon.1 = (f32[11,288,128]{2,1,0:T(8,128)S(1)}, bf16[11,288,128]{2,1,0:T(8,128)(2,1)S(1)}) custom-call(bf16[11,288,128]{2,1,0:T(8,128)(2,1)} %g_hbm.1, f32[11,288,128]{2,1,0:T(8,128)} %m_hbm.1), custom_call_target="tpu_custom_call" | custom-call | flops 1500000000 | bytes 5000000 | tf_op jit(solution)/shard_map/muon/pallas_call | solution.py:569
  57.3 1.2 %copy.6 = f32[11,288,128]{2,1,0:T(8,128)} copy(f32[11,288,128]{2,1,0:T(8,128)S(1)} %get-tuple-element.4) | data formatting | bytes 3244032
  58.5 0.9 %copy.7 = bf16[11,288,128]{2,1,0:T(8,128)(2,1)} copy(bf16[11,288,128]{2,1,0:T(8,128)(2,1)S(1)} %get-tuple-element.5) | data formatting | bytes 1622016

commit v3 on v2

--- a/solution.py
+++ b/solution.py
@@ -158,10 +158,6 @@
     def load_m(i):
         return pltpu.make_async_copy(m_hbm.at[i], mbuf.at[i], m_sem.at[i])
 
-    @pl.loop(0, MATS)
-    def _(i):
-        load_g(i).start()
-
     barrier = pltpu.get_barrier_semaphore()
 
     def greet(target):
@@ -177,6 +173,10 @@
         greet(dev((x + o // 4) % 4, (y + o) % 4, c))
 
     greet(partner)
+
+    @pl.loop(0, MATS)
+    def _(i):
+        load_g(i).start()
 
     def squares(i, total):
         load_g(i).wait()
@@ -319,11 +319,6 @@
             @pl.when(ym != y)
             def _():
                 s1_y(j, ym).start()
-
-    @pl.loop(0, MATS)
-    def _(i):
-        nmbuf[i] = DECAY * mbuf[i] + gbuf[i].astype(F32) * clip
-        store_nm(i).start()
 
     def s2_x(j, ym):
         k = slot(y, ym)
@@ -455,6 +450,11 @@
 
     @pl.loop(0, MATS)
     def _(i):
+        nmbuf[i] = DECAY * mbuf[i] + gbuf[i].astype(F32) * clip
+        store_nm(i).start()
+
+    @pl.loop(0, MATS)
+    def _(i):
         store_nm(i).wait()
 
     @pl.loop(1, 16)
@@ -524,8 +524,8 @@
             result = (dot(full[0], value) + dot(full[1], value)).astype(BF16)
             obuf[j, 0] = result[:, :128]
             obuf[j, 1] = result[:, 128:]
+            o_copy(j).start()
             o_local(j).start()
-            o_copy(j).start()
 
     @pl.loop(0, HALF)
     def _(j):

time: 59.5 us -> 59.2 us (level)
  no operation moved by 1% of the time
where the time goes in v3:
time: 59.2 us; the launch traced here: 59.1 us
  Pallas kernels  56.4 us (95%)
  local copies, waits for them, and re-layouts  2.05 us (3%)
  between operations  0.64 us (1%)
    pallas_call x1, Pallas kernels, per_device(): pl.pallas_call(kernel, out_shape=(jax.ShapeDtypeStruct((MATS, ROWS, COLS)...  56.4 us
    unnamed x2, local copies, waits for them, and re-layouts  2.05 us

profile of v3, /device:TPU:1, one launch (start us, length us, event | category | flops | bytes accessed | tf_op | source)
XLA Modules:
  0.0 59.1 jit_solution(7929514537888549517)
XLA Ops:
  0.6 56.4 %muon.1 = (f32[11,288,128]{2,1,0:T(8,128)S(1)}, bf16[11,288,128]{2,1,0:T(8,128)(2,1)S(1)}) custom-call(bf16[11,288,128]{2,1,0:T(8,128)(2,1)} %g_hbm.1, f32[11,288,128]{2,1,0:T(8,128)} %m_hbm.1), custom_call_target="tpu_custom_call" | custom-call | flops 1500000000 | bytes 5000000 | tf_op jit(solution)/shard_map/muon/pallas_call | solution.py:569
  57.0 1.2 %copy.6 = f32[11,288,128]{2,1,0:T(8,128)} copy(f32[11,288,128]{2,1,0:T(8,128)S(1)} %get-tuple-element.4) | data formatting | bytes 3244032
  58.2 0.9 %copy.7 = bf16[11,288,128]{2,1,0:T(8,128)(2,1)} copy(bf16[11,288,128]{2,1,0:T(8,128)(2,1)S(1)} %get-tuple-element.5) | data formatting | bytes 1622016

commit v4 on v3

--- a/solution.py
+++ b/solution.py
@@ -520,11 +520,9 @@
             cross = jnp.concatenate([first[128:176], second[0:80]], axis=0)
             unpack(gf, first[0:128], cross, second[80:112], second[112:144], second[144:176])
             full = split(gf[...])
-            value = jnp.concatenate([xx[j, 0], xx[j, 1]], axis=1)
-            result = (dot(full[0], value) + dot(full[1], value)).astype(BF16)
-            obuf[j, 0] = result[:, :128]
-            obuf[j, 1] = result[:, 128:]
+            obuf[j, 1] = (dot(full[0], xx[j, 1]) + dot(full[1], xx[j, 1])).astype(BF16)
             o_copy(j).start()
+            obuf[j, 0] = (dot(full[0], xx[j, 0]) + dot(full[1], xx[j, 0])).astype(BF16)
             o_local(j).start()
 
     @pl.loop(0, HALF)

time: 59.2 us -> 60.2 us (1.017)
  Pallas kernels: 56.4 us -> 57.4 us
    pallas_call x1, Pallas kernels: 56.4 us -> 57.4 us  [per_device(): pl.pallas_call(kernel, out_shape=(jax.ShapeDtypeStruct((MATS, ROWS, COLS)...]
where the time goes in v4:
time: 60.2 us; the launch traced here: 60.1 us
  Pallas kernels  57.4 us (95%)
  local copies, waits for them, and re-layouts  2.05 us (3%)
  between operations  0.64 us (1%)
    pallas_call x1, Pallas kernels, per_device(): pl.pallas_call(kernel, out_shape=(jax.ShapeDtypeStruct((MATS, ROWS, COLS)...  57.4 us
    unnamed x2, local copies, waits for them, and re-layouts  2.05 us

profile of v4, /device:TPU:1, one launch (start us, length us, event | category | flops | bytes accessed | tf_op | source)
XLA Modules:
  0.0 60.1 jit_solution(8869616551302031242)
XLA Ops:
  0.6 57.4 %muon.1 = (f32[11,288,128]{2,1,0:T(8,128)S(1)}, bf16[11,288,128]{2,1,0:T(8,128)(2,1)S(1)}) custom-call(bf16[11,288,128]{2,1,0:T(8,128)(2,1)} %g_hbm.1, f32[11,288,128]{2,1,0:T(8,128)} %m_hbm.1), custom_call_target="tpu_custom_call" | custom-call | flops 1500000000 | bytes 5000000 | tf_op jit(solution)/shard_map/muon/pallas_call | solution.py:567
  58.0 1.2 %copy.6 = f32[11,288,128]{2,1,0:T(8,128)} copy(f32[11,288,128]{2,1,0:T(8,128)S(1)} %get-tuple-element.4) | data formatting | bytes 3244032
  59.2 0.9 %copy.7 = bf16[11,288,128]{2,1,0:T(8,128)(2,1)} copy(bf16[11,288,128]{2,1,0:T(8,128)(2,1)S(1)} %get-tuple-element.5) | data formatting | bytes 1622016
